TPU v7x, 32 devices: a whole 2x2x4 slice. The times are simulated.
32 devices in a mesh: dp: 2 (over y), seq: 16 (over z, x, core).
Axes of the slice: x: 2, y: 2, z: 4, core: 2. Of those that a mesh axis runs over, the one named last changes fastest.
Arguments:
- tokens: bfloat16 [2, 4096, 768], P('dp', 'seq'), may hold values from -6 to 6
- segment_ids: int32 [2, 4096], P('dp', 'seq'), may hold values from 0 to 7, never falling along the last dimension, each value on 1 to 2048 neighbouring positions
- features: bfloat16 [12, 64, 256], replicated, may hold values from -6 to 6
- query_weight: bfloat16 [768, 768], replicated, may hold values from -0.15625 to 0.15625
- key_weight: bfloat16 [768, 768], replicated, may hold values from -0.15625 to 0.15625
- value_weight: bfloat16 [768, 768], replicated, may hold values from -0.21875 to 0.21875
- out_weight: bfloat16 [768, 768], replicated, may hold values from -0.875 to 0.875
- up_weight: bfloat16 [768, 3072], replicated, may hold values from -0.21875 to 0.21875
- down_weight: bfloat16 [3072, 768], replicated, may hold values from -0.109375 to 0.109375
- first_gain: float32 [768], replicated, may hold values from 0.1 to 1.9
- first_bias: float32 [768], replicated, may hold values from -3 to 3
- second_gain: float32 [768], replicated, may hold values from 0.1 to 1.9
- second_bias: float32 [768], replicated, may hold values from -3 to 3
- cotangent: bfloat16 [2, 4096, 768], P('dp', 'seq'), may hold values from -6 to 6
Outputs:
- output: bfloat16 [2, 4096, 768], P('dp', 'seq')
- grad_tokens: bfloat16 [2, 4096, 768], P('dp', 'seq')
- grad_query: float32 [768, 768], replicated
- grad_key: float32 [768, 768], replicated
- grad_value: float32 [768, 768], replicated
- grad_out: float32 [768, 768], replicated
- grad_up: float32 [768, 3072], replicated
- grad_down: float32 [3072, 768], replicated
- grad_first_gain: float32 [768], replicated
- grad_first_bias: float32 [768], replicated
- grad_second_gain: float32 [768], replicated
- grad_second_bias: float32 [768], replicated
Inputs may be any that keep to these rules, and one draw needn't show every extreme that they name: `segment_ids`: in each row the ids never fall, every id from 0 to 7 occurs, each on 1 to 2048 positions, and one on exactly 2048.
All inputs are finite; a program needn't handle non-finite values.
Results may differ from a plain program's by a relative error of at most 0.02.
Values sent between devices are 32-bit elements; how exact they have to be, the bound alone decides.
No kernel may reach another device: no remote copies, remote signals or barrier semaphores. Data moves between devices by JAX's collectives and lax.ppermute only.
A program may use at most 320 MiB of HBM per device.

v0:
```python
from functools import partial

import jax
import jax.numpy as jnp
from jax import lax
from jax.sharding import PartitionSpec as P

SEGS = 8


EPSILON = 1e-06
HIGHEST = lax.Precision.HIGHEST


def carried_in(value, axis, combine, identity, reverse):
    length, place = (lax.axis_size(axis), lax.axis_index(axis))
    everything = jax.tree.map(lambda part: lax.all_gather(part, axis), value)
    start = jax.tree.map(
        lambda part, zero: jnp.broadcast_to(jnp.asarray(zero, part.dtype), part.shape),
        value,
        identity,
    )

    def hop(k, before):
        at = length - 1 - k if reverse else k
        reached = at > place if reverse else at < place
        new = combine(before, jax.tree.map(lambda part: part[at], everything))
        return jax.tree.map(lambda a, b: jnp.where(reached, a, b), new, before)

    return lax.fori_loop(0, length, hop, start)


def norm_forward(hidden, norm_gain, norm_bias):
    row_mean = jnp.mean(hidden, -1, keepdims=True)
    centered = hidden - row_mean
    variance = jnp.mean(centered * centered, -1, keepdims=True)
    inv_std = lax.rsqrt(variance + EPSILON)
    normed = centered * inv_std
    return (normed * norm_gain + norm_bias, normed, inv_std)


def norm_backward(upstream, normed, inv_std, norm_gain):
    scaled = upstream * norm_gain
    grad_hidden = inv_std * (
        scaled
        - jnp.mean(scaled, -1, keepdims=True)
        - normed * jnp.mean(scaled * normed, -1, keepdims=True)
    )
    return (grad_hidden, jnp.sum(upstream * normed, 0), jnp.sum(upstream, 0))


def feature_map(projected, features):
    head_dim = projected.shape[-1]
    feat_count = features.shape[-1]
    inner_u = jnp.einsum("rthe,hem->rthm", projected, features, preferred_element_type=jnp.float32)
    widened = projected.astype(jnp.float32)
    square = jnp.sum(widened * widened, -1, keepdims=True)
    return jnp.exp(
        inner_u * head_dim ** (-0.25) - 0.5 * head_dim ** (-0.5) * square
    ) * feat_count ** (-0.5)


def feature_back(grad_feat, feat_vals, projected, features):
    head_dim = projected.shape[-1]
    weighted = grad_feat * feat_vals
    grad_inner = (weighted * head_dim ** (-0.25)).astype(jnp.bfloat16)
    grad_proj = jnp.einsum(
        "rthm,hem->rthe", grad_inner, features, preferred_element_type=jnp.float32
    )
    grad_proj = grad_proj - head_dim ** (-0.5) * projected.astype(jnp.float32) * jnp.sum(
        weighted, -1, keepdims=True
    )
    return grad_proj.astype(jnp.bfloat16)


def join_forward(earlier, later):
    earlier_kv, earlier_z, earlier_first, earlier_last, earlier_whole = earlier
    later_kv, later_z, later_first, later_last, later_whole = later
    matched = (earlier_last == later_first) | (earlier_last < 0) | (later_first < 0)
    joined = (later_whole == 1) & matched
    kv_part = jnp.where(joined[:, None, None, None], earlier_kv + later_kv, later_kv)
    z_part = jnp.where(joined[:, None, None], earlier_z + later_z, later_z)
    first_id = jnp.where(earlier_first < 0, later_first, earlier_first)
    last_id = jnp.where(later_last < 0, earlier_last, later_last)
    whole_run = earlier_whole * later_whole * matched.astype(jnp.int32)
    return (kv_part, z_part, first_id, last_id, whole_run)


def join_backward(earlier, later):
    earlier_kv, earlier_z, earlier_first, earlier_last, earlier_whole = earlier
    later_kv, later_z, later_first, later_last, later_whole = later
    matched = (later_last == earlier_first) | (later_last < 0) | (earlier_first < 0)
    joined = (later_whole == 1) & matched
    kv_part = jnp.where(joined[:, None, None, None], earlier_kv + later_kv, later_kv)
    z_part = jnp.where(joined[:, None, None], earlier_z + later_z, later_z)
    first_id = jnp.where(later_first < 0, earlier_first, later_first)
    last_id = jnp.where(earlier_last < 0, later_last, earlier_last)
    whole_run = earlier_whole * later_whole * matched.astype(jnp.int32)
    return (kv_part, z_part, first_id, last_id, whole_run)


def segment_totals(local_kv, local_z, segment_ids):
    row_count = local_kv.shape[0]
    labels = jnp.arange(local_kv.shape[1], dtype=jnp.int32)
    first_id = segment_ids[:, 0]
    last_id = segment_ids[:, -1]
    whole_run = (first_id == last_id).astype(jnp.int32)
    is_last = last_id[:, None] == labels[None, :]
    is_first = first_id[:, None] == labels[None, :]
    tail_kv = jnp.sum(jnp.where(is_last[:, :, None, None, None], local_kv, 0.0), 1)
    tail_z = jnp.sum(jnp.where(is_last[:, :, None, None], local_z, 0.0), 1)
    lead_kv = jnp.sum(jnp.where(is_first[:, :, None, None, None], local_kv, 0.0), 1)
    lead_z = jnp.sum(jnp.where(is_first[:, :, None, None], local_z, 0.0), 1)
    identity = (
        jnp.zeros_like(tail_kv),
        jnp.zeros_like(tail_z),
        -jnp.ones((row_count,), jnp.int32),
        -jnp.ones((row_count,), jnp.int32),
        jnp.ones((row_count,), jnp.int32),
    )
    before = carried_in(
        (tail_kv, tail_z, first_id, last_id, whole_run), "seq", join_forward, identity, False
    )
    behind = carried_in(
        (lead_kv, lead_z, first_id, last_id, whole_run), "seq", join_backward, identity, True
    )
    from_before = before[3][:, None] == labels[None, :]
    from_behind = behind[2][:, None] == labels[None, :]
    total_kv = (
        local_kv
        + jnp.where(from_before[:, :, None, None, None], before[0][:, None], 0.0)
        + jnp.where(from_behind[:, :, None, None, None], behind[0][:, None], 0.0)
    )
    total_z = (
        local_z
        + jnp.where(from_before[:, :, None, None], before[1][:, None], 0.0)
        + jnp.where(from_behind[:, :, None, None], behind[1][:, None], 0.0)
    )
    return (total_kv, total_z)


def body(
    tokens,
    segment_ids,
    features,
    query_weight,
    key_weight,
    value_weight,
    out_weight,
    up_weight,
    down_weight,
    first_gain,
    first_bias,
    second_gain,
    second_bias,
    cotangent,
):
    row_count, row_len, width_d = tokens.shape
    head_count, head_dim = (features.shape[0], features.shape[1])
    token_count = row_count * row_len
    tokens_flat = tokens.reshape(token_count, width_d)

    def project(weight):
        product = jnp.dot(tokens_flat, weight, preferred_element_type=jnp.float32)
        return product.astype(jnp.bfloat16).reshape(row_count, row_len, head_count, head_dim)

    queries = project(query_weight)
    keys_b = project(key_weight)
    values_b = project(value_weight)
    feat_q = feature_map(queries, features)
    feat_k = feature_map(keys_b, features)
    feat_q_b = feat_q.astype(jnp.bfloat16)
    feat_k_b = feat_k.astype(jnp.bfloat16)
    labels = jnp.arange(SEGS, dtype=jnp.int32)
    onehot = segment_ids[:, :, None] == labels[None, None, :]
    mask_b = onehot.astype(jnp.bfloat16)
    mask_f = onehot.astype(jnp.float32)
    masked_values = mask_b[:, :, :, None, None] * values_b[:, :, None]
    local_kv = jnp.einsum(
        "rthm,rtshe->rshme", feat_k_b, masked_values, preferred_element_type=jnp.float32
    )
    local_z = jnp.einsum("rts,rthm->rshm", mask_b, feat_k_b, preferred_element_type=jnp.float32)
    kv_total, z_total = segment_totals(local_kv, local_z, segment_ids)
    kv_b = kv_total.astype(jnp.bfloat16)
    per_segment = jnp.einsum(
        "rthm,rshme->rtshe", feat_q_b, kv_b, preferred_element_type=jnp.float32
    )
    numer = jnp.sum(jnp.where(onehot[:, :, :, None, None], per_segment, 0.0), 2)
    z_picked = jnp.einsum("rts,rshm->rthm", mask_f, z_total, precision=HIGHEST)
    denom = jnp.sum(feat_q_b.astype(jnp.float32) * z_picked, -1)
    attention = numer / denom[..., None]
    attention_b = attention.astype(jnp.bfloat16).reshape(token_count, width_d)
    hidden_one = tokens_flat.astype(jnp.float32) + jnp.dot(
        attention_b, out_weight, preferred_element_type=jnp.float32
    )
    normed_one, unit_one, inv_one = norm_forward(hidden_one, first_gain, first_bias)
    normed_one_b = normed_one.astype(jnp.bfloat16)
    inner_f = jnp.dot(normed_one_b, up_weight, preferred_element_type=jnp.float32)
    activated, gelu_pull = jax.vjp(partial(jax.nn.gelu, approximate=False), inner_f)
    activated_b = activated.astype(jnp.bfloat16)
    hidden_two = normed_one + jnp.dot(activated_b, down_weight, preferred_element_type=jnp.float32)
    result, unit_two, inv_two = norm_forward(hidden_two, second_gain, second_bias)
    upstream = cotangent.reshape(token_count, width_d).astype(jnp.float32)
    grad_two, grad_gain_two, grad_bias_two = norm_backward(upstream, unit_two, inv_two, second_gain)
    grad_branch = grad_two.astype(jnp.bfloat16)
    grad_down_w = jnp.einsum(
        "nf,nd->fd", activated_b, grad_branch, preferred_element_type=jnp.float32
    )
    grad_act = jnp.einsum("nd,fd->nf", grad_branch, down_weight, preferred_element_type=jnp.float32)
    (grad_inner,) = gelu_pull(grad_act)
    grad_inner_b = grad_inner.astype(jnp.bfloat16)
    grad_up_w = jnp.einsum(
        "nd,nf->df", normed_one_b, grad_inner_b, preferred_element_type=jnp.float32
    )
    grad_normed = grad_two + jnp.einsum(
        "nf,df->nd", grad_inner_b, up_weight, preferred_element_type=jnp.float32
    )
    grad_one, grad_gain_one, grad_bias_one = norm_backward(
        grad_normed, unit_one, inv_one, first_gain
    )
    grad_attn_out = grad_one.astype(jnp.bfloat16)
    grad_out_w = jnp.einsum(
        "nd,ne->de", attention_b, grad_attn_out, preferred_element_type=jnp.float32
    )
    grad_attention = jnp.einsum(
        "ne,de->nd", grad_attn_out, out_weight, preferred_element_type=jnp.float32
    )
    grad_attention = grad_attention.reshape(row_count, row_len, head_count, head_dim)
    grad_numer_b = (grad_attention / denom[..., None]).astype(jnp.bfloat16)
    grad_denom = -jnp.sum(grad_attention * attention, -1) / denom
    masked_grad = mask_b[:, :, :, None, None] * grad_numer_b[:, :, None]
    grad_feat_q = jnp.einsum(
        "rtshe,rshme->rthm", masked_grad, kv_b, preferred_element_type=jnp.float32
    )
    grad_feat_q = grad_feat_q + z_picked * grad_denom[..., None]
    local_grad_kv = jnp.einsum(
        "rthm,rtshe->rshme", feat_q_b, masked_grad, preferred_element_type=jnp.float32
    )
    local_grad_z = jnp.einsum(
        "rts,rthm->rshm",
        mask_f,
        feat_q_b.astype(jnp.float32) * grad_denom[..., None],
        precision=HIGHEST,
    )
    grad_kv_total, grad_z_total = segment_totals(local_grad_kv, local_grad_z, segment_ids)
    grad_kv_b = grad_kv_total.astype(jnp.bfloat16)
    grad_feat_k = jnp.einsum(
        "rtshe,rshme->rthm", masked_values, grad_kv_b, preferred_element_type=jnp.float32
    )
    grad_feat_k = grad_feat_k + jnp.einsum(
        "rts,rshm->rthm", mask_f, grad_z_total, precision=HIGHEST
    )
    value_terms = jnp.einsum(
        "rthm,rshme->rtshe", feat_k_b, grad_kv_b, preferred_element_type=jnp.float32
    )
    grad_values = jnp.sum(jnp.where(onehot[:, :, :, None, None], value_terms, 0.0), 2).astype(
        jnp.bfloat16
    )
    grad_queries = feature_back(grad_feat_q, feat_q, queries, features)
    grad_keys = feature_back(grad_feat_k, feat_k, keys_b, features)
    grad_q_flat = grad_queries.reshape(token_count, width_d)
    grad_k_flat = grad_keys.reshape(token_count, width_d)
    grad_v_flat = grad_values.reshape(token_count, width_d)
    grad_query_w = jnp.einsum(
        "nd,ne->de", tokens_flat, grad_q_flat, preferred_element_type=jnp.float32
    )
    grad_key_w = jnp.einsum(
        "nd,ne->de", tokens_flat, grad_k_flat, preferred_element_type=jnp.float32
    )
    grad_value_w = jnp.einsum(
        "nd,ne->de", tokens_flat, grad_v_flat, preferred_element_type=jnp.float32
    )
    grad_input = (
        grad_one
        + jnp.einsum("ne,de->nd", grad_q_flat, query_weight, preferred_element_type=jnp.float32)
        + jnp.einsum("ne,de->nd", grad_k_flat, key_weight, preferred_element_type=jnp.float32)
        + jnp.einsum("ne,de->nd", grad_v_flat, value_weight, preferred_element_type=jnp.float32)
    )
    local_grads = (
        grad_query_w,
        grad_key_w,
        grad_value_w,
        grad_out_w,
        grad_up_w,
        grad_down_w,
        grad_gain_one,
        grad_bias_one,
        grad_gain_two,
        grad_bias_two,
    )
    shares = (
        lax.psum_scatter(local_grads[0], "seq", scatter_dimension=0, tiled=True),
        lax.psum_scatter(local_grads[1], "seq", scatter_dimension=0, tiled=True),
        lax.psum_scatter(local_grads[2], "seq", scatter_dimension=0, tiled=True),
        lax.psum_scatter(local_grads[3], "seq", scatter_dimension=0, tiled=True),
        lax.psum_scatter(local_grads[4], "seq", scatter_dimension=0, tiled=True),
        lax.psum_scatter(local_grads[5], "seq", scatter_dimension=0, tiled=True),
        lax.psum_scatter(local_grads[6], "seq", scatter_dimension=0, tiled=True),
        lax.psum_scatter(local_grads[7], "seq", scatter_dimension=0, tiled=True),
        lax.psum_scatter(local_grads[8], "seq", scatter_dimension=0, tiled=True),
        lax.psum_scatter(local_grads[9], "seq", scatter_dimension=0, tiled=True),
    )
    shares = lax.psum(
        (
            shares[0],
            shares[1],
            shares[2],
            shares[3],
            shares[4],
            shares[5],
            shares[6],
            shares[7],
            shares[8],
            shares[9],
        ),
        "dp",
    )
    summed = (
        lax.all_gather(shares[0], "seq", axis=0, tiled=True),
        lax.all_gather(shares[1], "seq", axis=0, tiled=True),
        lax.all_gather(shares[2], "seq", axis=0, tiled=True),
        lax.all_gather(shares[3], "seq", axis=0, tiled=True),
        lax.all_gather(shares[4], "seq", axis=0, tiled=True),
        lax.all_gather(shares[5], "seq", axis=0, tiled=True),
        lax.all_gather(shares[6], "seq", axis=0, tiled=True),
        lax.all_gather(shares[7], "seq", axis=0, tiled=True),
        lax.all_gather(shares[8], "seq", axis=0, tiled=True),
        lax.all_gather(shares[9], "seq", axis=0, tiled=True),
    )
    return (
        result.astype(jnp.bfloat16).reshape(row_count, row_len, width_d),
        grad_input.astype(jnp.bfloat16).reshape(row_count, row_len, width_d),
        summed[0],
        summed[1],
        summed[2],
        summed[3],
        summed[4],
        summed[5],
        summed[6],
        summed[7],
        summed[8],
        summed[9],
    )


def solution(mesh):
    placed = (
        P("dp", "seq", None),
        P("dp", "seq"),
        P(),
        P(),
        P(),
        P(),
        P(),
        P(),
        P(),
        P(),
        P(),
        P(),
        P(),
        P("dp", "seq", None),
    )
    return jax.shard_map(
        body,
        mesh=mesh,
        in_specs=placed,
        out_specs=(
            P("dp", "seq", None),
            P("dp", "seq", None),
            P(),
            P(),
            P(),
            P(),
            P(),
            P(),
            P(),
            P(),
            P(),
            P(),
        ),
        check_vma=False,
    )
```

profile of v0, /device:TPU:0, one launch (start us, length us, event | category | flops | bytes accessed | tf_op | source)
XLA Modules:
  0.0 1856.2 jit_solution(2164421294902823707)
XLA Ops:
  17.5 5.5 fusion.14
  29.0 14.5 all-reduce.11
  51.3 21.1 %all-gather.9 = f32[16,12,256]{2,1,0:T(8,128)} all-gather(f32[1,12,256]{2,1,0:T(8,128)S(1)} %bitcast.471), channel_id=5, replica_groups=mesh['dp'=2,'seq'=16] {'seq'}, dimensions={0}, use_global_device_ids=true | all-gather | bytes 208896 | tf_op jit(solution)/shard_map/all_gather | solution.py:17
  72.4 21.7 %all-gather.8 = f32[16,12,256]{2,1,0:T(8,128)} all-gather(f32[1,12,256]{2,1,0:T(8,128)S(1)} %bitcast.470), channel_id=3, replica_groups=mesh['dp'=2,'seq'=16] {'seq'}, dimensions={0}, use_global_device_ids=true | all-gather | bytes 208896 | tf_op jit(solution)/shard_map/all_gather | solution.py:17
  97.1 33.2 %all-gather.37.cloned.1.call-done = f32[192,256,64]{1,2,0:T(8,128)} async-done(((f32[12,256,64]{1,2,0:T(8,128)}), f32[192,256,64]{1,2,0:T(8,128)}) %all-gather.37.cloned.1.call-update) | async-done | bytes 12582928 | tf_op jit(solution)/shard_map/all_gather | solution.py:17
  130.2 174.4 %while.77 = (s32[]{:T(128)}, f32[1,12,256,64]{3,2,1,0:T(8,128)}, f32[1,12,256]{2,1,0:T(8,128)}, s32[1]{0:T(128)}, s32[]{:T(128)}, /*index=5*/s32[16,1]{0,1:T(1,1...) while((s32[]{:T(128)}, f32[1,12,256,64]{3,2,1,0:T(8,128)}, ...), condition=%wide.region_8.9_spmd.clone, body=%wide.region_7.8_spmd.clone.sunk | while | flops 798738 | bytes 5640575 | solution.py:30
  307.4 174.1 %while.76 = (s32[]{:T(128)}, f32[1,12,256,64]{3,2,1,0:T(8,128)}, f32[1,12,256]{2,1,0:T(8,128)S(1)}, s32[1]{0:T(128)}, s32[]{:T(128)}, /*index=5*/s32[16,1]{0,1:T...) while((s32[]{:T(128)}, f32[1,12,256,64]{3,2,1,0:T(8,128)}, ...), condition=%wide.region_4.5_spmd.clone, body=%wide.region_3.4_spmd.clone.sunk | while | flops 798734 | bytes 5542153 | solution.py:30
  483.5 4.4 fusion.31
  494.8 8.1 multiply_convert_fusion.2
  514.5 5.5 fusion.10
  520.9 5.8 fusion.172
  535.6 22.5 %all-gather.11 = f32[16,12,256]{2,1,0:T(8,128)} all-gather(f32[1,12,256]{2,1,0:T(8,128)S(1)} %bitcast.469), channel_id=9, replica_groups=mesh['dp'=2,'seq'=16] {'seq'}, dimensions={0}, use_global_device_ids=true | all-gather | bytes 208896 | tf_op jit(solution)/shard_map/all_gather | solution.py:17
  558.1 20.6 %all-gather.10 = f32[16,12,256]{2,1,0:T(8,128)} all-gather(f32[1,12,256]{2,1,0:T(8,128)S(1)} %bitcast.468), channel_id=7, replica_groups=mesh['dp'=2,'seq'=16] {'seq'}, dimensions={0}, use_global_device_ids=true | all-gather | bytes 208896 | tf_op jit(solution)/shard_map/all_gather | solution.py:17
  578.8 43.1 %all-gather.41.cloned.1.call-done = f32[192,256,64]{1,2,0:T(8,128)} async-done(((f32[12,256,64]{1,2,0:T(8,128)}), f32[192,256,64]{1,2,0:T(8,128)}) %all-gather.41.cloned.1.call-update) | async-done | bytes 12582928 | tf_op jit(solution)/shard_map/all_gather | solution.py:17
  621.9 172.3 %while.79 = (s32[]{:T(128)}, f32[1,12,256,64]{3,2,1,0:T(8,128)}, f32[1,12,256]{2,1,0:T(8,128)}, s32[1]{0:T(128)}, s32[]{:T(128)}, /*index=5*/s32[16,1]{0,1:T(1,1...) while((s32[]{:T(128)}, f32[1,12,256,64]{3,2,1,0:T(8,128)}, ...), condition=%wide.region_29.30_spmd.clone, body=%wide.region_28.29_spmd.clone.sunk | while | flops 798738 | bytes 5640575 | solution.py:30
  794.2 171.2 %while.78 = (s32[]{:T(128)}, f32[1,12,256,64]{3,2,1,0:T(8,128)}, f32[1,12,256]{2,1,0:T(8,128)S(1)}, s32[1]{0:T(128)}, s32[]{:T(128)}, /*index=5*/s32[16,1]{0,1:T...) while((s32[]{:T(128)}, f32[1,12,256,64]{3,2,1,0:T(8,128)}, ...), condition=%wide.region_25.26_spmd.clone, body=%wide.region_24.25_spmd.clone.sunk | while | flops 798734 | bytes 5542153 | solution.py:30
  971.3 4.2 fusion.32
  994.8 6.8 fusion.156
  1003.4 6.1 fusion.116
  1011.4 34.0 %reduce-scatter.21.cloned.1.call-done = f32[48,768]{1,0:T(8,128)} async-done(((f32[768,768]{1,0:T(8,128)}), f32[48,768]{1,0:T(8,128)}) %reduce-scatter.21.cloned.1.call-update) | async-done | bytes 147472
  1047.2 64.5 %reduce-scatter.23.cloned.1.call-done = f32[48,768]{1,0:T(8,128)} async-done(((f32[768,768]{1,0:T(8,128)}), f32[48,768]{1,0:T(8,128)}) %reduce-scatter.23.cloned.1.call-update) | async-done | bytes 147472
  1113.6 65.0 %reduce-scatter.13.cloned.1.call-done = f32[48,768]{1,0:T(8,128)} async-done(((f32[768,768]{1,0:T(8,128)}), f32[48,768]{1,0:T(8,128)}) %reduce-scatter.13.cloned.1.call-update) | async-done | bytes 147472 | tf_op jit(solution)/shard_map/reduce_scatter | solution.py:295
  1178.6 115.1 %reduce-scatter.15.cloned.1.call-done = f32[48,3072]{1,0:T(8,128)} async-done(((f32[768,3072]{1,0:T(8,128)}), f32[48,3072]{1,0:T(8,128)}) %reduce-scatter.15.cloned.1.call-update) | async-done | bytes 589840 | tf_op jit(solution)/shard_map/reduce_scatter | solution.py:296
  1293.7 116.2 %reduce-scatter.17.cloned.1.call-done = f32[192,768]{1,0:T(8,128)} async-done(((f32[3072,768]{1,0:T(8,128)}), f32[192,768]{1,0:T(8,128)}) %reduce-scatter.17.cloned.1.call-update) | async-done | bytes 589840 | tf_op jit(solution)/shard_map/reduce_scatter | solution.py:297
  1410.0 75.6 %all-reduce.18.cloned.1.call-done = (f32[48,768]{0,1:T(8,128)}, f32[48,768]{0,1:T(8,128)}, f32[48,768]{0,1:T(8,128)}, f32[48,768]{1,0:T(8,128)}, f32[48,3072]{1,0:T(8,128)}, /*index=5*/f32[192,768]{1,0:T(8,128)}) async-done(((f32[48,768]{0,1:T(8,128)}, f32[48,768]{0,1:T(8,128)}, f32[48,768]{0,1:T(8,128)}, f32[48,768]{1,0:T(8,128)}, f32[48,3072]{1,0:T(8,128)}, /*index=5*/f32[192,768]{1,0:T(8,128)}), ...) | async-done | bytes 1769488 | tf_op jit(solution)/shard_map/psum | solution.py:303
  1495.5 61.4 %all-reduce.13 = (f32[768]{0:T(1024)}, f32[768]{0:T(1024)}, f32[768]{0:T(1024)}, f32[768]{0:T(1024)}) all-reduce(f32[768]{0:T(1024)S(1)} %copy-done.94, f32[768]{0:T(1024)S(1)} %copy-done.95, f32[768]{0:T(1024)S(1)} %copy-done.76, f32[768]{0:T(1024)S(1)} %convert_reduce_fusion), channel_id=16, replica_groups=mesh['dp'=2,'seq'=16] {'seq'}, use_global_device_ids=true, to_apply=%region_45.46.clone | all-reduce | flops 3072 | bytes 24576
  1559.9 5.4 all-reduce.14
  1568.7 57.9 %all-reduce.12 = (f32[768]{0:T(1024)}, f32[768]{0:T(1024)}, f32[768]{0:T(1024)}, f32[768]{0:T(1024)}) all-reduce(f32[768]{0:T(1024)S(1)} %dynamic-update-slice.3, f32[768]{0:T(1024)S(1)} %dynamic-update-slice.4, f32[768]{0:T(1024)S(1)} %dynamic-update-slice.5, f32[768]{0:T(1024)S(1)} %dynamic-update-slice.6), channel_id=1, replica_groups=mesh['dp'=2,'seq'=16] {'seq'}, use_global_device_ids=true, to_apply=%add.3 | all-reduce | flops 3072 | bytes 24576
  1629.4 33.7 %all-gather.29.cloned.1.call-done = f32[768,768]{1,0:T(8,128)} async-done(((f32[48,768]{1,0:T(8,128)}), f32[768,768]{1,0:T(8,128)}) %all-gather.29.cloned.1.call-update) | async-done | bytes 2359312 | tf_op jit(solution)/shard_map/all_gather | solution.py:322
  1663.1 82.7 %all-gather.31.cloned.1.call-done = f32[768,3072]{1,0:T(8,128)} async-done(((f32[48,3072]{1,0:T(8,128)}), f32[768,3072]{1,0:T(8,128)}) %all-gather.31.cloned.1.call-update) | async-done | bytes 9437200 | tf_op jit(solution)/shard_map/all_gather | solution.py:323
  1745.7 82.0 %all-gather.33.cloned.1.call-done = f32[3072,768]{1,0:T(8,128)} async-done(((f32[192,768]{1,0:T(8,128)}), f32[3072,768]{1,0:T(8,128)}) %all-gather.33.cloned.1.call-update) | async-done | bytes 9437200 | tf_op jit(solution)/shard_map/all_gather | solution.py:324
  1841.1 8.1 copy.216
  (858 shorter events, 608.3 us)
Async XLA Ops:
  7.2 485.6 %copy-start = (bf16[768,768]{1,0:T(8,128)(2,1)S(1)}, bf16[768,768]{1,0:T(8,128)(2,1)}, u32[]{:S(2)}) copy-start(bf16[768,768]{1,0:T(8,128)(2,1)} %param.28) | copy-start | bytes 3538948
  7.2 123.0 %all-gather.37.cloned.1.call-start = ((), (), s32[]{:S(2)}) async-start(), calls=%async_computation.16 | async-start | bytes 13369344 | tf_op jit(solution)/shard_map/all_gather | solution.py:17
  23.0 26.4 %copy-start.18 = (bf16[1,256,12,256]{1,3,2,0:T(8,128)(2,1)S(1)}, bf16[1,256,12,256]{1,3,2,0:T(8,128)(2,1)}, u32[]{:S(2)}) copy-start(bf16[1,256,12,256]{1,3,2,0:T(8,128)(2,1)} %copy-done.17) | copy-start | bytes 4718596
  23.0 284.4 %all-gather.35.cloned.1.call-start = ((), (), s32[]{:S(2)}) async-start(), calls=%async_computation.15 | async-start | bytes 13369344 | tf_op jit(solution)/shard_map/all_gather | solution.py:17
  23.8 598.1 %all-gather.41.cloned.1.call-start = ((), (), s32[]{:S(2)}) async-start(), calls=%async_computation.18 | async-start | bytes 13369344 | tf_op jit(solution)/shard_map/all_gather | solution.py:17
  47.2 49.9 %copy-start.15 = (f32[256,768]{0,1:T(8,128)}, f32[256,768]{0,1:T(8,128)S(1)}, u32[]{:S(2)}) copy-start(f32[256,768]{0,1:T(8,128)S(1)} %copy.83) | copy-start | bytes 2359300
  49.4 45.4 %copy-start.23 = (bf16[12,64,256]{2,1,0:T(8,128)(2,1)S(1)}, bf16[12,64,256]{2,1,0:T(8,128)(2,1)}, u32[]{:S(2)}) copy-start(bf16[12,64,256]{2,1,0:T(8,128)(2,1)} %param.24) | copy-start | bytes 1179652
  49.4 45.4 %copy-start.46 = (bf16[256,768]{0,1:T(8,128)(2,1)S(1)}, bf16[256,768]{0,1:T(8,128)(2,1)}, u32[]{:S(2)}) copy-start(bf16[256,768]{0,1:T(8,128)(2,1)} %copy.82) | copy-start | bytes 1179652
  491.6 22.7 %copy-start.52 = (f32[256,12]{0,1:T(8,128)}, f32[256,12]{0,1:T(8,128)S(1)}, u32[]{:S(2)}) copy-start(f32[256,12]{0,1:T(8,128)S(1)} %get-tuple-element.1168) | copy-start | bytes 36868
  491.6 22.8 %copy-start.20 = (bf16[1,256,12,256]{1,3,2,0:T(8,128)(2,1)}, bf16[1,256,12,256]{1,3,2,0:T(8,128)(2,1)S(1)}, u32[]{:S(2)}) copy-start(bf16[1,256,12,256]{1,3,2,0:T(8,128)(2,1)S(1)} %get-tuple-element.1169) | copy-start | bytes 4718596
  493.7 19.0 %copy-start.8 = (f32[256,768]{1,0:T(8,128)}, f32[256,768]{1,0:T(8,128)S(1)}, u32[]{:S(2)}) copy-start(f32[256,768]{1,0:T(8,128)S(1)} %get-tuple-element.1191) | copy-start | bytes 2359300
  520.1 274.2 %all-gather.39.cloned.1.call-start = ((), (), s32[]{:S(2)}) async-start(), calls=%async_computation.17 | async-start | bytes 13369344 | tf_op jit(solution)/shard_map/all_gather | solution.py:17
  520.6 488.9 %reduce-scatter.19.cloned.1.call-start = ((), (), s32[]{:S(2)}) async-start(), calls=%async_computation.19 | async-start | bytes 2506752
  578.8 466.6 %reduce-scatter.21.cloned.1.call-start = ((), (), s32[]{:S(2)}) async-start(), calls=%async_computation.20 | async-start | bytes 2506752
  983.6 128.1 %reduce-scatter.23.cloned.1.call-start = ((), (), s32[]{:S(2)}) async-start(), calls=%async_computation.21 | async-start | bytes 2506752
  992.5 186.1 %reduce-scatter.13.cloned.1.call-start = ((), (), s32[]{:S(2)}) async-start(), calls=%async_computation.9 | async-start | bytes 2506752 | tf_op jit(solution)/shard_map/reduce_scatter | solution.py:295
  994.7 299.0 %reduce-scatter.15.cloned.1.call-start = ((), (), s32[]{:S(2)}) async-start(), calls=%async_computation.11 | async-start | bytes 10027008 | tf_op jit(solution)/shard_map/reduce_scatter | solution.py:296
  1001.6 408.3 %reduce-scatter.17.cloned.1.call-start = ((), (), s32[]{:S(2)}) async-start(), calls=%async_computation.13 | async-start | bytes 10027008 | tf_op jit(solution)/shard_map/reduce_scatter | solution.py:297
  1009.4 476.2 %all-reduce.18.cloned.1.call-start = ((), (), s32[]{:S(2)}) async-start(), calls=%async_computation.22 | async-start | bytes 5013504 | tf_op jit(solution)/shard_map/psum | solution.py:303
  1409.9 85.5 %copy-start.76 = (f32[768]{0:T(1024)S(1)}, f32[768]{0:T(1024)}, u32[]{:S(2)}) copy-start(f32[768]{0:T(1024)} %get-tuple-element.1056) | copy-start | bytes 9220
  1409.9 85.5 %copy-start.94 = (f32[768]{0:T(1024)S(1)}, f32[768]{0:T(1024)}, u32[]{:S(2)}) copy-start(f32[768]{0:T(1024)} %get-tuple-element.1054) | copy-start | bytes 9220
  1409.9 85.5 %copy-start.95 = (f32[768]{0:T(1024)S(1)}, f32[768]{0:T(1024)}, u32[]{:S(2)}) copy-start(f32[768]{0:T(1024)} %get-tuple-element.1059) | copy-start | bytes 9220
  1409.9 216.6 %copy-start.25 = (bf16[768,768]{1,0:T(8,128)(2,1)S(1)}, bf16[768,768]{1,0:T(8,128)(2,1)}, u32[]{:S(2)}) copy-start(bf16[768,768]{1,0:T(8,128)(2,1)} %param.25) | copy-start | bytes 3538948
  1410.0 216.6 %copy-start.29 = (bf16[1,256,12,64]{1,3,2,0:T(8,128)(2,1)S(1)}, bf16[1,256,12,64]{1,3,2,0:T(8,128)(2,1)}, u32[]{:S(2)}) copy-start(bf16[1,256,12,64]{1,3,2,0:T(8,128)(2,1)} %copy-done.28) | copy-start | bytes 1179652
  1410.0 219.4 %all-gather.23.cloned.1.call-start = ((), (), s32[]{:S(2)}) async-start(), calls=%async_computation.6 | async-start | bytes 2506752 | tf_op jit(solution)/shard_map/all_gather | solution.py:319
  1487.5 141.9 %all-gather.25.cloned.1.call-start = ((), (), s32[]{:S(2)}) async-start(), calls=%async_computation.7 | async-start | bytes 2506752 | tf_op jit(solution)/shard_map/all_gather | solution.py:320
  1487.6 139.6 %copy-start.26 = (bf16[768,768]{1,0:T(8,128)(2,1)S(1)}, bf16[768,768]{1,0:T(8,128)(2,1)}, u32[]{:S(2)}) copy-start(bf16[768,768]{1,0:T(8,128)(2,1)} %param.26) | copy-start | bytes 3538948
  1489.5 139.9 %all-gather.27.cloned.1.call-start = ((), (), s32[]{:S(2)}) async-start(), calls=%async_computation.8 | async-start | bytes 2506752 | tf_op jit(solution)/shard_map/all_gather | solution.py:321
  1491.4 171.7 %all-gather.29.cloned.1.call-start = ((), (), s32[]{:S(2)}) async-start(), calls=%async_computation.10 | async-start | bytes 2506752 | tf_op jit(solution)/shard_map/all_gather | solution.py:322
  1492.0 253.8 %all-gather.31.cloned.1.call-start = ((), (), s32[]{:S(2)}) async-start(), calls=%async_computation.12 | async-start | bytes 10027008 | tf_op jit(solution)/shard_map/all_gather | solution.py:323
  1492.5 335.2 %all-gather.33.cloned.1.call-start = ((), (), s32[]{:S(2)}) async-start(), calls=%async_computation.14 | async-start | bytes 10027008 | tf_op jit(solution)/shard_map/all_gather | solution.py:324
  1629.4 201.7 %copy-start.40 = (f32[768,768]{1,0:T(8,128)S(1)}, f32[768,768]{1,0:T(8,128)}, u32[]{:S(2)}) copy-start(f32[768,768]{1,0:T(8,128)} %all-gather.25.cloned.1.call-done) | copy-start | bytes 7077892
  (148 other events, 603.8 us)
Sparse Core Ops, SparseCore 0:
  23.2 107.0 all-gather.36
  133.1 98.9 all-gather.34
  520.2 101.6 all-gather.40
  624.1 99.2 all-gather.38
  727.6 61.1 reduce-scatter.18
  983.7 61.6 reduce-scatter.20
  1049.7 61.9 reduce-scatter.22
  1116.6 61.9 reduce-scatter.12
  1183.3 110.3 reduce-scatter.14
  1298.8 111.1 reduce-scatter.16
  1413.2 72.4 all-reduce.17
  1488.6 42.2 all-gather.22
  1534.1 41.1 all-gather.24
  1578.3 41.0 all-gather.26
  1621.8 41.2 all-gather.28
  1665.5 80.2 all-gather.30
  1748.1 79.5 all-gather.32
where the time goes:
time: 1880 us; the launch traced here: 1860 us
  waiting for transfers between devices  748 us (40%)
  other arithmetic  311 us (17%)
  local copies, waits for them, and re-layouts  263 us (14%)
  blocking collectives  225 us (12%)
  loops' own time  205 us (11%)
  matrix products  84.1 us (4%)
    select_n x128, other arithmetic, hop(): return jax.tree.map(lambda a, b: jnp.where(reached, a, b), new, before)  219 us
    another operation x4, loops' own time, carried_in(): return lax.fori_loop(0, length, hop, start)  205 us
    dynamic_slice x192, local copies, waits for them, and re-layouts, hop(): new = combine(before, jax.tree.map(lambda part: part[at], everything))  191 us
    unnamed x3, blocking collectives  134 us
    reduce_scatter x1, waiting for transfers between devices, body(): lax.psum_scatter(local_grads[5], 'seq', scatter_dimension=0, tiled=True)  116 us
    reduce_scatter x1, waiting for transfers between devices, body(): lax.psum_scatter(local_grads[4], 'seq', scatter_dimension=0, tiled=True)  115 us
    unnamed x20, waiting for transfers between devices  102 us
    all_gather x4, blocking collectives, carried_in(): everything = jax.tree.map(lambda part: lax.all_gather(part, axis), value)  85.9 us
  transfers between devices with their start and end apart: 17, of which 11 were waited for; matrix products, arithmetic and copies ran while one was open for 25% of the time, Pallas kernels for 0%

commit v1 on v0

v1 whole, which is shorter than its diff:
```python
from functools import partial

import jax
import jax.numpy as jnp
from jax import lax
from jax.sharding import PartitionSpec as P

SEG_MOST = 2048
EPSILON = 1e-06
AXES = ("dp", "seq")
BF = jnp.bfloat16
F32 = jnp.float32


def mm(a, b):
    return jnp.dot(a, b, preferred_element_type=F32)


def mm_nt(a, b):
    return lax.dot_general(a, b, (((1,), (1,)), ((), ())), preferred_element_type=F32)


def mm_tn(a, b):
    return lax.dot_general(a, b, (((0,), (0,)), ((), ())), preferred_element_type=F32)


def dslice(a, start, size, axis=0):
    return lax.dynamic_slice_in_dim(a, start, size, axis)


class Net:
    def __init__(self, n_dp, n_seq):
        self.n_dp, self.n_seq = n_dp, n_seq
        self.nz = 4
        self.nx = n_seq // 8
        self.fast = n_dp == 2 and n_seq == 16
        seq = lax.axis_index("seq")
        self.y = lax.axis_index("dp")
        self.core = seq % 2
        self.x = (seq // 2) % self.nx
        self.z = seq // (2 * self.nx)
        self.seq = seq
        self.one = jnp.where(seq < 0, 0.5, 1.0).astype(F32)

    def perm(self, move):
        pairs = []
        for y in range(self.n_dp):
            for s in range(self.n_seq):
                target = move(y, s // (2 * self.nx), (s // 2) % self.nx, s % 2)
                if target is not None:
                    ty, tz, tx, tc = target
                    pairs.append((y * self.n_seq + s, ty * self.n_seq + (tz * self.nx + tx) * 2 + tc))
        return pairs

    def send(self, value, move):
        return lax.ppermute(value, AXES, self.perm(move))

    def over_core(self, value):
        return self.send(value, lambda y, z, x, c: (y, z, x, 1 - c))

    def swap_b(self, value):
        got = self.over_core(value.astype(F32))
        return (got * self.one).astype(BF)

    def over_x(self, value, inner=False):
        return self.send(
            value, lambda y, z, x, c: None if inner and z in (0, 3) else (y, z, 1 - x, c)
        )

    def over_y(self, value, inner=False):
        return self.send(
            value, lambda y, z, x, c: None if inner and z in (0, 3) else (1 - y, z, x, c)
        )

    def z_up(self, value):
        return self.send(value, lambda y, z, x, c: (y, z + 1, x, c) if z < 3 else None)

    def z_down(self, value):
        return self.send(value, lambda y, z, x, c: (y, z - 1, x, c) if z > 0 else None)

    def z_in(self, value):
        return self.send(
            value, lambda y, z, x, c: (y, (1, 1, 2, 2)[z], x, c) if z in (0, 3) else None
        )

    def z_out(self, value):
        return self.send(
            value, lambda y, z, x, c: (y, (0, 0, 3, 3)[z], x, c) if z in (1, 2) else None
        )

    def z_swap(self, value):
        return self.send(value, lambda y, z, x, c: (y, 3 - z, x, c) if z in (1, 2) else None)

    def shift(self, value, step):
        chips = self.n_seq // 2
        pairs = []
        for y in range(self.n_dp):
            for s in range(self.n_seq):
                if 0 <= s // 2 + step < chips:
                    pairs.append((y * self.n_seq + s, y * self.n_seq + s + 2 * step))
        return lax.ppermute(value, AXES, pairs)


def keep_if(flag, value):
    return jnp.where(flag[:, None, None], value, 0.0)


def exchange(net, lead, tail, first, last, chip_len):
    rows = first.shape[0]
    if not net.fast:
        before = [jnp.zeros_like(part) for part in lead]
        behind = [jnp.zeros_like(part) for part in lead]
        up = (tail, last)
        down = (lead, first)
        for _ in range(min(net.n_seq // 2 - 1, -(-SEG_MOST // chip_len))):
            up = jax.tree.map(lambda part: net.shift(part, 1), up)
            down = jax.tree.map(lambda part: net.shift(part, -1), down)
            before = [b + keep_if(up[1] == first, part) for b, part in zip(before, up[0])]
            behind = [b + keep_if(down[1] == last, part) for b, part in zip(behind, down[0])]
        return before, behind
    at_one = net.x == 1

    def pick(pair, flag):
        return jnp.where(flag, pair[1], pair[0])

    ids = jnp.stack([first, last])
    ids_other = net.over_x(ids)
    mine = [pick(lead, at_one), pick(tail, at_one)]
    theirs = [net.over_x(pick(lead, ~at_one)), net.over_x(pick(tail, ~at_one))]
    lead0, lead1 = jnp.where(at_one, theirs[0], mine[0]), jnp.where(at_one, mine[0], theirs[0])
    tail0, tail1 = jnp.where(at_one, theirs[1], mine[1]), jnp.where(at_one, mine[1], theirs[1])
    first0, first1 = jnp.where(at_one, ids_other[0], first), jnp.where(at_one, first, ids_other[0])
    last0, last1 = jnp.where(at_one, ids_other[1], last), jnp.where(at_one, last, ids_other[1])
    up = tail1 + keep_if(last0 == last1, tail0)
    down = lead0 + keep_if(first1 == first0, lead1)
    up_id, down_id = last1, first0
    before = jnp.zeros_like(up)
    behind = jnp.zeros_like(up)
    for _ in range(min(net.nz - 1, -(-SEG_MOST // (2 * chip_len)))):
        up, up_id = net.z_up(up), net.z_up(up_id)
        down, down_id = net.z_down(down), net.z_down(down_id)
        before = before + keep_if(up_id == first0, up)
        behind = behind + keep_if(down_id == last1, down)
    before0, behind1 = before, behind
    behind0 = keep_if(last0 == first1, lead1) + keep_if(last0 == last1, behind)
    before1 = keep_if(first1 == last0, tail0) + keep_if(first1 == first0, before)
    own_before = jnp.where(at_one, before1, before0)
    own_behind = jnp.where(at_one, behind1, behind0)
    got_before = net.over_x(jnp.where(at_one, before0, before1))
    got_behind = net.over_x(jnp.where(at_one, behind0, behind1))
    befores = [jnp.where(at_one, got_before, own_before), jnp.where(at_one, own_before, got_before)]
    behinds = [jnp.where(at_one, got_behind, own_behind), jnp.where(at_one, own_behind, got_behind)]
    return befores, behinds


def pair_scatter(value, place, move):
    half = value.shape[0] // 2
    got = move(dslice(value, (1 - place) * half, half))
    return dslice(value, place * half, half) + got


def pair_gather(value, place, move):
    got = move(value)
    flag = place == 0
    return jnp.concatenate([jnp.where(flag, value, got), jnp.where(flag, got, value)], 0)


def all_reduce(net, value, order):
    z_side = jnp.where(net.z >= 2, 1, 0)
    inner = (net.z == 1) | (net.z == 2)
    seen_z = False
    for axis in order:
        if axis == "z":
            value = value + net.z_in(value)
            value = pair_scatter(value, z_side, net.z_swap)
            seen_z = True
        elif axis == "x":
            value = pair_scatter(value, net.x, partial(net.over_x, inner=seen_z))
        else:
            value = pair_scatter(value, net.y, partial(net.over_y, inner=seen_z))
    for axis in order[::-1]:
        if axis == "z":
            value = pair_gather(value, z_side, net.z_swap)
            got = net.z_out(value)
            value = jnp.where(inner, value, got)
            seen_z = False
        elif axis == "x":
            value = pair_gather(value, net.x, partial(net.over_x, inner=seen_z))
        else:
            value = pair_gather(value, net.y, partial(net.over_y, inner=seen_z))
    return value


def small_sum(net, value):
    if not net.fast:
        return lax.psum(value, AXES)
    value = value + net.over_core(value)
    value = value + net.over_x(value)
    value = value + net.over_y(value)
    value = value + net.send(value, lambda y, z, x, c: (y, z ^ 1, x, c))
    return value + net.send(value, lambda y, z, x, c: (y, z ^ 2, x, c))


def join_cores(net, half, axis):
    got = net.over_core(half)
    flag = net.core == 0
    return jnp.concatenate([jnp.where(flag, half, got), jnp.where(flag, got, half)], axis)


def total(net, half, axis, parts):
    if not net.fast:
        size = half.shape[axis]
        shape = tuple(2 * n if i == axis else n for i, n in enumerate(half.shape))
        own = lax.dynamic_update_slice_in_dim(
            jnp.zeros(shape, F32), half, net.core * size, axis
        )
        return lax.psum(own, AXES)
    pieces = []
    at = 0
    for count, order in parts:
        pieces.append(join_cores(net, all_reduce(net, half[at : at + count], order), axis))
        at += count
    if axis == 1:
        return jnp.concatenate(pieces, 0)
    half_rows = half.shape[0]
    low, high = [], []
    for piece in pieces:
        n = piece.shape[0] // 2
        low.append(piece[:n])
        high.append(piece[n:])
    return jnp.concatenate(low + high, 0)


def norm_forward(hidden, norm_gain, norm_bias):
    row_mean = jnp.mean(hidden, -1, keepdims=True)
    centered = hidden - row_mean
    variance = jnp.mean(centered * centered, -1, keepdims=True)
    inv_std = lax.rsqrt(variance + EPSILON)
    normed = centered * inv_std
    return (normed * norm_gain + norm_bias, normed, inv_std)


def norm_backward(upstream, normed, inv_std, norm_gain):
    scaled = upstream * norm_gain
    grad_hidden = inv_std * (
        scaled
        - jnp.mean(scaled, -1, keepdims=True)
        - normed * jnp.mean(scaled * normed, -1, keepdims=True)
    )
    return (grad_hidden, jnp.sum(upstream * normed, 0), jnp.sum(upstream, 0))


def heads_of(flat, heads):
    rows, length, width = flat.shape
    return flat.reshape(rows, length, heads, width // heads)


def feature_map(projected, features):
    head_dim = projected.shape[-1]
    feat_count = features.shape[-1]
    inner_u = jnp.einsum("rthe,hem->rhtm", projected, features, preferred_element_type=F32)
    widened = projected.astype(F32)
    square = jnp.sum(widened * widened, -1).transpose(0, 2, 1)[..., None]
    return jnp.exp(
        inner_u * head_dim ** (-0.25) - 0.5 * head_dim ** (-0.5) * square
    ) * feat_count ** (-0.5)


def feature_back(grad_feat, feat_vals, projected, features):
    head_dim = projected.shape[-1]
    weighted = grad_feat * feat_vals
    grad_inner = (weighted * head_dim ** (-0.25)).astype(BF)
    grad_proj = jnp.einsum("rhtm,hem->rthe", grad_inner, features, preferred_element_type=F32)
    folded = jnp.sum(weighted, -1).transpose(0, 2, 1)[..., None]
    grad_proj = grad_proj - head_dim ** (-0.5) * projected.astype(F32) * folded
    return grad_proj.astype(BF)


def edge_sums(values, weights, feats, lead_mask, tail_mask):
    rows, length, heads, head_dim = values.shape
    feat_count = feats.shape[-1]
    out = []
    for mask in (lead_mask, tail_mask):
        masked = jnp.where(mask[:, :, None, None], values, jnp.zeros((), values.dtype))
        sums = jnp.einsum("rthe,rhtm->rhem", masked, feats, preferred_element_type=F32)
        scaled = jnp.where(mask[:, :, None], weights, 0.0)
        zs = jnp.einsum("rth,rhtm->rhm", scaled, feats.astype(F32), precision=lax.Precision.HIGHEST)
        groups = []
        half = heads // 2
        for g in range(2):
            part = sums[:, g * half : (g + 1) * half].reshape(rows, half * head_dim, feat_count)
            pad = jnp.zeros((rows, 8 - half, feat_count), F32)
            groups.append(jnp.concatenate([part, zs[:, g * half : (g + 1) * half], pad], 1))
        out.append(groups)
    return out


def split_carry(groups, heads, head_dim):
    rows = groups[0].shape[0]
    half = heads // 2
    kv = jnp.concatenate(
        [g[:, : half * head_dim].reshape(rows, half, head_dim, -1) for g in groups], 1
    )
    zs = jnp.concatenate([g[:, half * head_dim : half * head_dim + half] for g in groups], 1)
    return kv, zs


def body(
    tokens,
    segment_ids,
    features,
    query_weight,
    key_weight,
    value_weight,
    out_weight,
    up_weight,
    down_weight,
    first_gain,
    first_bias,
    second_gain,
    second_bias,
    cotangent,
):
    net = Net(lax.axis_size("dp"), lax.axis_size("seq"))
    rows, length, width = tokens.shape
    heads_all, head_dim, feat_count = features.shape
    heads = heads_all // 2
    mine = width // 2
    core = net.core
    chip_len = 2 * length
    count = rows * length

    tokens_other = net.swap_b(tokens)
    x_chip = jnp.concatenate([tokens, tokens_other], 1)
    ids = segment_ids.astype(F32)
    ids_chip = jnp.concatenate([ids, net.over_core(ids)], 1)
    first = jnp.min(ids_chip, 1)
    last = jnp.max(ids_chip, 1)
    lead_mask = ids_chip == first[:, None]
    tail_mask = ids_chip == last[:, None]
    same = (ids_chip[:, :, None] == ids_chip[:, None, :])[:, None]
    lead_f = lead_mask.astype(F32)[:, None, :, None]
    tail_f = tail_mask.astype(F32)[:, None, :, None]

    feats = dslice(features, core * heads, heads)
    wq = dslice(query_weight, core * mine, mine, 1)
    wk = dslice(key_weight, core * mine, mine, 1)
    wv = dslice(value_weight, core * mine, mine, 1)
    wo = dslice(out_weight, core * mine, mine, 0)
    wo_other = dslice(out_weight, (1 - core) * mine, mine, 0)
    x_flat = x_chip.reshape(rows * chip_len, width)

    def project(weight):
        return heads_of(mm(x_flat, weight).astype(BF).reshape(rows, chip_len, mine), heads)

    keys_b = project(wk)
    values_b = project(wv)
    feat_k = feature_map(keys_b, feats)
    feat_k_b = feat_k.astype(BF)
    ones = jnp.ones((rows, chip_len, heads), F32)
    lead, tail = edge_sums(values_b, ones, feat_k_b, lead_mask, tail_mask)
    before, behind = exchange(net, lead, tail, first, last, chip_len)
    queries = project(wq)
    feat_q = feature_map(queries, feats)
    feat_q_b = feat_q.astype(BF)
    scores = jnp.einsum("rhtm,rhsm->rhts", feat_q_b, feat_k_b, preferred_element_type=F32)
    scores = jnp.where(same, scores, 0.0)
    scores_b = scores.astype(BF)
    numer = jnp.einsum("rhts,rshe->rhte", scores_b, values_b, preferred_element_type=F32)
    denom = jnp.sum(scores, -1, keepdims=True)

    kv_before, z_before = split_carry(before, heads, head_dim)
    kv_behind, z_behind = split_carry(behind, heads, head_dim)
    kv_before_b, kv_behind_b = kv_before.astype(BF), kv_behind.astype(BF)
    wide_q = feat_q_b.astype(F32)

    def carried(left, kv):
        return jnp.einsum("rhtm,rhem->rhte", left, kv, preferred_element_type=F32)

    numer = numer + lead_f * carried(feat_q_b, kv_before_b) + tail_f * carried(feat_q_b, kv_behind_b)
    z_picked = lead_f * z_before[:, :, None, :] + tail_f * z_behind[:, :, None, :]
    denom = denom + jnp.sum(wide_q * z_picked, -1, keepdims=True)
    attention = numer / denom
    attention_b = attention.astype(BF).transpose(0, 2, 1, 3).reshape(rows, chip_len, mine)
    attn_mine = attention_b[:, :length].reshape(count, mine)
    attn_got = net.swap_b(attention_b[:, length:]).reshape(count, mine)

    tokens_flat = tokens.reshape(count, width)
    hidden_one = tokens_flat.astype(F32) + mm(attn_mine, wo) + mm(attn_got, wo_other)
    normed_one, unit_one, inv_one = norm_forward(hidden_one, first_gain, first_bias)
    normed_one_b = normed_one.astype(BF)
    y1_other = net.swap_b(normed_one_b)
    inner_f = mm(normed_one_b, up_weight)
    activated, gelu_pull = jax.vjp(partial(jax.nn.gelu, approximate=False), inner_f)
    activated_b = activated.astype(BF)
    ff_half = up_weight.shape[1] // 2
    act_mine = dslice(activated_b, core * ff_half, ff_half, 1)
    act_other = net.swap_b(dslice(activated_b, (1 - core) * ff_half, ff_half, 1))
    hidden_two = normed_one + mm(activated_b, down_weight)
    result, unit_two, inv_two = norm_forward(hidden_two, second_gain, second_bias)
    upstream = cotangent.reshape(count, width).astype(F32)
    grad_two, grad_gain_two, grad_bias_two = norm_backward(upstream, unit_two, inv_two, second_gain)
    grad_branch = grad_two.astype(BF)
    gz_other = net.swap_b(grad_branch)
    grad_act = mm_nt(grad_branch, down_weight)
    (grad_inner,) = gelu_pull(grad_act)
    grad_inner_b = grad_inner.astype(BF)
    gi_mine = dslice(grad_inner_b, core * ff_half, ff_half, 1)
    gi_other = net.swap_b(dslice(grad_inner_b, (1 - core) * ff_half, ff_half, 1))

    def both(a, b):
        return jnp.concatenate([a, b], 0)

    y1_chip = both(normed_one_b, y1_other)
    act_chip = both(act_mine, act_other)
    gz_chip = both(grad_branch, gz_other)
    gi_chip = both(gi_mine, gi_other)
    grad_up_half = mm_tn(y1_chip, gi_chip)
    grad_down_half = mm_tn(act_chip, gz_chip)
    grad_up = total(net, grad_up_half, 1, [(256, "xyz"), (256, "yxz"), (256, "zxy")])
    grad_down = total(
        net, grad_down_half, 0, [(384, "xyz"), (384, "yxz"), (384, "zyx"), (384, "zxy")]
    )

    grad_normed = grad_two + mm_nt(grad_inner_b, up_weight)
    grad_one, grad_gain_one, grad_bias_one = norm_backward(grad_normed, unit_one, inv_one, first_gain)
    grad_o = grad_one.astype(BF).reshape(rows, length, width)
    go_chip = jnp.concatenate([grad_o, net.swap_b(grad_o)], 1)
    go_flat = go_chip.reshape(rows * chip_len, width)
    grad_out_half = mm_tn(attention_b.reshape(rows * chip_len, mine), go_flat)
    grad_out = total(net, grad_out_half, 0, [(384, "zyx")])

    grad_att = mm_nt(go_flat, wo).reshape(rows, chip_len, mine)
    grad_att = heads_of(grad_att, heads).transpose(0, 2, 1, 3)
    grad_numer = (grad_att / denom).astype(BF)
    grad_denom = -jnp.sum(grad_att * attention, -1, keepdims=True) / denom
    lead_d, tail_d = edge_sums(
        grad_numer.transpose(0, 2, 1, 3), grad_denom[..., 0].transpose(0, 2, 1), feat_q_b, lead_mask, tail_mask
    )
    before_d, behind_d = exchange(net, lead_d, tail_d, first, last, chip_len)
    pulls = jnp.einsum("rhte,rshe->rhts", grad_numer, values_b, preferred_element_type=F32)
    pulls_b = jnp.where(same, pulls + grad_denom, 0.0).astype(BF)
    grad_feat_q = jnp.einsum("rhts,rhsm->rhtm", pulls_b, feat_k_b, preferred_element_type=F32)

    def pulled(left, kv):
        return jnp.einsum("rhte,rhem->rhtm", left, kv, preferred_element_type=F32)

    grad_feat_q = (
        grad_feat_q
        + lead_f * pulled(grad_numer, kv_before_b)
        + tail_f * pulled(grad_numer, kv_behind_b)
        + grad_denom * z_picked
    )
    grad_queries = feature_back(grad_feat_q, feat_q, queries, feats).reshape(rows * chip_len, mine)
    grad_query_half = mm_tn(x_flat, grad_queries)
    grad_query = total(net, grad_query_half, 1, [(768, "xyz")])

    dkv_before, dz_before = split_carry(before_d, heads, head_dim)
    dkv_behind, dz_behind = split_carry(behind_d, heads, head_dim)
    dkv_before_b, dkv_behind_b = dkv_before.astype(BF), dkv_behind.astype(BF)
    values_t = values_b.transpose(0, 2, 1, 3)
    grad_feat_k = jnp.einsum("rhts,rhtm->rhsm", pulls_b, feat_q_b, preferred_element_type=F32)
    grad_feat_k = (
        grad_feat_k
        + lead_f * (pulled(values_t, dkv_before_b) + dz_before[:, :, None, :])
        + tail_f * (pulled(values_t, dkv_behind_b) + dz_behind[:, :, None, :])
    )
    grad_values = jnp.einsum("rhts,rhte->rhse", scores_b, grad_numer, preferred_element_type=F32)
    grad_values = (
        grad_values
        + lead_f * carried(feat_k_b, dkv_before_b)
        + tail_f * carried(feat_k_b, dkv_behind_b)
    )
    grad_values = grad_values.astype(BF).transpose(0, 2, 1, 3).reshape(rows * chip_len, mine)
    grad_keys = feature_back(grad_feat_k, feat_k, keys_b, feats).reshape(rows * chip_len, mine)
    grad_key = total(net, mm_tn(x_flat, grad_keys), 1, [(768, "yxz")])
    grad_value = total(net, mm_tn(x_flat, grad_values), 1, [(768, "zxy")])

    shares = mm_nt(grad_queries, wq) + mm_nt(grad_keys, wk) + mm_nt(grad_values, wv)
    shares = shares.reshape(rows, chip_len, width)
    grad_input = (
        grad_one.reshape(rows, length, width)
        + shares[:, :length]
        + net.over_core(shares[:, length:])
    )
    small = small_sum(
        net, jnp.stack([grad_gain_one, grad_bias_one, grad_gain_two, grad_bias_two])
    )
    return (
        result.astype(BF).reshape(rows, length, width),
        grad_input.astype(BF),
        grad_query,
        grad_key,
        grad_value,
        grad_out,
        grad_up,
        grad_down,
        small[0],
        small[1],
        small[2],
        small[3],
    )


def solution(mesh):
    split = P("dp", "seq", None)
    placed = (split, P("dp", "seq")) + (P(),) * 11 + (split,)
    return jax.shard_map(
        body,
        mesh=mesh,
        in_specs=placed,
        out_specs=(split, split) + (P(),) * 10,
        check_vma=False,
    )
```

time: 1880 us -> 849 us (0.45)
  waiting for transfers between devices: 748 us -> 436 us
  starting transfers between devices: 0.94 us -> 284 us
  other arithmetic: 311 us -> 44.2 us
  local copies, waits for them, and re-layouts: 263 us -> 11.7 us
  blocking collectives: 225 us -> 0 us
  loops' own time: 205 us -> 0 us
  matrix products: 84.1 us -> 53.3 us
    ppermute x0 -> x134, waiting for transfers between devices: none -> 436 us  [send(): return lax.ppermute(value, AXES, self.perm(move))]
    reduce_scatter x3 -> x0, waiting for transfers between devices: 296 us -> none  [the longest x1 116 us: body(): lax.psum_scatter(local_grads[5], 'seq', scatter_dimension=0, tiled=True)]
    ppermute x0 -> x134, starting transfers between devices: none -> 284 us  [send(): return lax.ppermute(value, AXES, self.perm(move))]
    all_gather x10 -> x0, waiting for transfers between devices: 275 us -> none  [the longest x1 82.7 us: body(): lax.all_gather(shares[4], 'seq', axis=0, tiled=True)]
    select_n x128 -> x67, other arithmetic: 219 us -> 5.97 us  [the longest x33 1.93 us: pair_gather(): jnp.where(flag, value, got)]
    another operation x4 -> x0, loops' own time: 205 us -> none  [carried_in(): return lax.fori_loop(0, length, hop, start)]
    dynamic_slice x192 -> x34, local copies, waits for them, and re-layouts: 191 us -> 1.2 us  [dslice(): return lax.dynamic_slice_in_dim(a, start, size, axis)]
    unnamed x3 -> x0, blocking collectives: 134 us -> none
  transfers between devices with their start and end apart: 17 -> 134, of which waited for: 11 -> 51; matrix products, arithmetic and copies ran while one was open for 25% -> 7% of each run, Pallas kernels for 0% -> 0%
where the time goes in v1:
time: 849 us; the launch traced here: 841 us
  waiting for transfers between devices  436 us (51%)
  starting transfers between devices  284 us (33%)
  matrix products  53.3 us (6%)
  other arithmetic  44.2 us (5%)
  between operations  12.3 us (1%)
  local copies, waits for them, and re-layouts  11.7 us (1%)
    ppermute x134, waiting for transfers between devices, send(): return lax.ppermute(value, AXES, self.perm(move))  436 us
    ppermute x134, starting transfers between devices, send(): return lax.ppermute(value, AXES, self.perm(move))  284 us
  transfers between devices with their start and end apart: 134, of which 51 were waited for; matrix products, arithmetic and copies ran while one was open for 7% of the time, Pallas kernels for 0%

profile of v1, /device:TPU:0, one launch (start us, length us, event | category | flops | bytes accessed | tf_op | source)
XLA Modules:
  0.0 841.4 jit_solution(894449147862487373)
XLA Ops:
  16.5 5.3 collective-permute-start.3
  80.7 5.7 collective-permute-done.11
  87.9 6.2 collective-permute-done.13
  94.9 5.1 collective-permute-done.14
  111.6 9.4 %multiply_convert_fusion.2 = (bf16[256,3072]{1,0:T(8,128)(2,1)S(1)}, f32[256,3072]{1,0:T(8,128)S(1)}, f32[256,3072]{1,0:T(8,128)S(1)}) fusion(bf16[256,768]{1,0:T(8,128)(2,1)S(1)} %get-tuple-element.30, bf16[768,3072]{1,0:T(8,128)(2,1)S(1)} %bitcast.441), kind=kOutput, calls=%fused_computation.19 | convolution fusion | flops 1259077632 | bytes 12976128 | tf_op jit(solution)/shard_map/dot_general | solution.py:16
  175.2 7.2 collective-permute-done.22
  192.4 25.6 %collective-permute-start.82 = (f32[256,1536]{1,0:T(8,128)S(1)}, f32[256,1536]{1,0:T(8,128)S(1)}, u32[]{:S(2)}, u32[]{:S(2)}) collective-permute-start(f32[256,1536]{1,0:T(8,128)S(1)} %slice.248), channel_id=1, source_target_pairs={{0,4},{1,5},{2,6},{3,7},{12,8},{13,9},{14,10},{15,11},{16,20},{17,... | collective-permute-start | bytes 4718600 | tf_op jit(solution)/shard_map/ppermute | solution.py:56
  228.6 55.1 %collective-permute-done.28 = f32[192,384]{1,0:T(8,128)S(1)} collective-permute-done((f32[192,384]{1,0:T(8,128)S(1)}, f32[192,384]{1,0:T(8,128)S(1)}, u32[]{:S(2)}, u32[]{:S(2)}) %collective-permute-start.28) | collective-permute-done | bytes 294944 | tf_op jit(solution)/shard_map/ppermute | solution.py:56
  284.6 5.7 collective-permute-start.111
  292.0 4.9 collective-permute-start.19
  296.9 19.0 %collective-permute-done.19 = f32[1,200,256]{2,1,0:T(8,128)S(1)} collective-permute-done((f32[1,200,256]{2,1,0:T(8,128)S(1)}, f32[1,200,256]{2,1,0:T(8,128)S(1)}, u32[]{:S(2)}, u32[]{:S(2)}) %collective-permute-start.19) | collective-permute-done | bytes 204832 | tf_op jit(solution)/shard_map/ppermute | solution.py:56
  338.9 8.1 collective-permute-start.44
  349.2 8.3 collective-permute-done.32
  364.9 14.0 %collective-permute-done.36 = f32[192,384]{1,0:T(8,128)S(1)} collective-permute-done((f32[192,384]{1,0:T(8,128)S(1)}, f32[192,384]{1,0:T(8,128)S(1)}, u32[]{:S(2)}, u32[]{:S(2)}) %collective-permute-start.36) | collective-permute-done | bytes 294944 | tf_op jit(solution)/shard_map/ppermute | solution.py:56
  384.6 8.5 %collective-permute-done.33 = f32[384,384]{1,0:T(8,128)S(1)} collective-permute-done((f32[384,384]{1,0:T(8,128)S(1)}, f32[384,384]{1,0:T(8,128)S(1)}, u32[]{:S(2)}, u32[]{:S(2)}) %collective-permute-start.33) | collective-permute-done | bytes 589856 | tf_op jit(solution)/shard_map/ppermute | solution.py:56
  393.1 40.9 %collective-permute-start.37 = (f32[192,384]{1,0:T(8,128)S(1)}, f32[192,384]{1,0:T(8,128)S(1)}, u32[]{:S(2)}, u32[]{:S(2)}) collective-permute-start(f32[192,384]{1,0:T(8,128)S(1)} %dynamic-slice_add_fusion.20), channel_id=1, source_target_pairs={{0,4},{1,5},{2,6},{3,7},{12,8},{13,9},{14,10},{15,11},{16,20},{17,... | collective-permute-start | bytes 884744 | tf_op jit(solution)/shard_map/ppermute | solution.py:56
  442.2 11.2 %collective-permute-done.103 = f32[96,768]{1,0:T(8,128)S(1)} collective-permute-done((f32[96,768]{1,0:T(8,128)S(1)}, f32[96,768]{1,0:T(8,128)S(1)}, u32[]{:S(2)}, u32[]{:S(2)}) %collective-permute-start.103) | collective-permute-done | bytes 294944 | tf_op jit(solution)/shard_map/ppermute | solution.py:56
  456.4 35.8 %collective-permute-start.95 = (f32[96,768]{1,0:T(8,128)S(1)}, f32[96,768]{1,0:T(8,128)S(1)}, u32[]{:S(2)}, u32[]{:S(2)}) collective-permute-start(f32[96,768]{1,0:T(8,128)S(1)} %dynamic-slice_add_fusion.17), channel_id=1, source_target_pairs={{0,4},{1,5},{2,6},{3,7},{12,8},{13,9},{14,10},{15,11},{16,20},{17,... | collective-permute-start | bytes 884744 | tf_op jit(solution)/shard_map/ppermute | solution.py:56
  493.8 13.8 %collective-permute-start.104 = (f32[96,768]{1,0:T(8,128)S(1)}, f32[96,768]{1,0:T(8,128)S(1)}, u32[]{:S(2)}, u32[]{:S(2)}) collective-permute-start(f32[96,768]{1,0:T(8,128)S(1)} %dynamic-slice_add_fusion.16), channel_id=1, source_target_pairs={{0,4},{1,5},{2,6},{3,7},{12,8},{13,9},{14,10},{15,11},{16,20},{17,... | collective-permute-start | bytes 884744 | tf_op jit(solution)/shard_map/ppermute | solution.py:56
  536.0 55.0 %collective-permute-done.98 = f32[96,768]{1,0:T(8,128)S(1)} collective-permute-done((f32[96,768]{1,0:T(8,128)S(1)}, f32[96,768]{1,0:T(8,128)S(1)}, u32[]{:S(2)}, u32[]{:S(2)}) %collective-permute-start.98) | collective-permute-done | bytes 294944 | tf_op jit(solution)/shard_map/ppermute | solution.py:56
  594.9 8.8 %collective-permute-start.75 = (f32[64,1536]{1,0:T(8,128)S(1)}, f32[64,1536]{1,0:T(8,128)S(1)}, u32[]{:S(2)}, u32[]{:S(2)}) collective-permute-start(f32[64,1536]{1,0:T(8,128)S(1)} %dynamic-slice_add_fusion.12), channel_id=1, source_target_pairs={{0,4},{1,5},{2,6},{3,7},{12,8},{13,9},{14,10},{15,11},{16,20},{17,... | collective-permute-start | bytes 1179656 | tf_op jit(solution)/shard_map/ppermute | solution.py:56
  606.9 14.5 %collective-permute-start.66 = (f32[64,1536]{1,0:T(8,128)S(1)}, f32[64,1536]{1,0:T(8,128)S(1)}, u32[]{:S(2)}, u32[]{:S(2)}) collective-permute-start(f32[64,1536]{1,0:T(8,128)S(1)} %dynamic-slice_add_fusion.13), channel_id=1, source_target_pairs={{0,4},{1,5},{2,6},{3,7},{12,8},{13,9},{14,10},{15,11},{16,20},{17,... | collective-permute-start | bytes 1179656 | tf_op jit(solution)/shard_map/ppermute | solution.py:56
  621.9 4.8 collective-permute-done.66
  627.8 12.7 %collective-permute-done.99 = f32[96,768]{1,0:T(8,128)S(1)} collective-permute-done((f32[96,768]{1,0:T(8,128)S(1)}, f32[96,768]{1,0:T(8,128)S(1)}, u32[]{:S(2)}, u32[]{:S(2)}) %collective-permute-start.99) | collective-permute-done | bytes 294944 | tf_op jit(solution)/shard_map/ppermute | solution.py:56
  664.3 64.9 %collective-permute-done.78 = f32[64,1536]{1,0:T(8,128)S(1)} collective-permute-done((f32[64,1536]{1,0:T(8,128)S(1)}, f32[64,1536]{1,0:T(8,128)S(1)}, u32[]{:S(2)}, u32[]{:S(2)}) %collective-permute-start.78) | collective-permute-done | bytes 393248 | tf_op jit(solution)/shard_map/ppermute | solution.py:56
  730.6 8.3 collective-permute-done.69
  740.2 11.3 %collective-permute-done.79 = f32[64,1536]{1,0:T(8,128)S(1)} collective-permute-done((f32[64,1536]{1,0:T(8,128)S(1)}, f32[64,1536]{1,0:T(8,128)S(1)}, u32[]{:S(2)}, u32[]{:S(2)}) %collective-permute-start.79) | collective-permute-done | bytes 393248 | tf_op jit(solution)/shard_map/ppermute | solution.py:56
  753.3 9.0 %collective-permute-done.70 = f32[64,1536]{1,0:T(8,128)S(1)} collective-permute-done((f32[64,1536]{1,0:T(8,128)S(1)}, f32[64,1536]{1,0:T(8,128)S(1)}, u32[]{:S(2)}, u32[]{:S(2)}) %collective-permute-start.70) | collective-permute-done | bytes 393248 | tf_op jit(solution)/shard_map/ppermute | solution.py:56
  772.4 15.2 %collective-permute-done.80 = f32[128,1536]{1,0:T(8,128)S(1)} collective-permute-done((f32[128,1536]{1,0:T(8,128)S(1)}, f32[128,1536]{1,0:T(8,128)S(1)}, u32[]{:S(2)}, u32[]{:S(2)}) %collective-permute-start.80) | collective-permute-done | bytes 786464 | tf_op jit(solution)/shard_map/ppermute | solution.py:56
  791.0 6.0 collective-permute-done.51
  798.7 31.4 %collective-permute-done.89 = f32[256,1536]{1,0:T(8,128)S(1)} collective-permute-done((f32[256,1536]{1,0:T(8,128)S(1)}, f32[256,1536]{1,0:T(8,128)S(1)}, u32[]{:S(2)}, u32[]{:S(2)}) %collective-permute-start.89) | collective-permute-done | bytes 1572896 | tf_op jit(solution)/shard_map/ppermute | solution.py:56
  834.0 7.1 maximum_maximum_fusion
  (719 shorter events, 290.2 us)
Async XLA Ops:
  146.3 44.5 %collective-permute-start.63 = (f32[256,1536]{1,0:T(8,128)S(1)}, f32[256,1536]{1,0:T(8,128)S(1)}, u32[]{:S(2)}, u32[]{:S(2)}) collective-permute-start(f32[256,1536]{1,0:T(8,128)S(1)} %get-tuple-element.84), channel_id=1, source_target_pairs={{0,1},{1,0},{2,3},{3,2},{4,5},{5,4},{6,7},{7,6},{8,9},{9,8},{10,11... | collective-permute-start | bytes 4718600 | tf_op jit(solution)/shard_map/ppermute | solution.py:56
  146.8 71.2 %collective-permute-start.91 = (f32[256,1536]{1,0:T(8,128)S(1)}, f32[256,1536]{1,0:T(8,128)S(1)}, u32[]{:S(2)}, u32[]{:S(2)}) collective-permute-start(f32[256,1536]{1,0:T(8,128)S(1)} %get-tuple-element.76), channel_id=1, source_target_pairs={{0,1},{1,0},{2,3},{3,2},{4,5},{5,4},{6,7},{7,6},{8,9},{9,8},{10,11... | collective-permute-start | bytes 4718600 | tf_op jit(solution)/shard_map/ppermute | solution.py:56
  169.7 114.8 %collective-permute-start.53 = (f32[384,768]{1,0:T(8,128)S(1)}, f32[384,768]{1,0:T(8,128)S(1)}, u32[]{:S(2)}, u32[]{:S(2)}) collective-permute-start(f32[384,768]{1,0:T(8,128)S(1)} %fusion.110), channel_id=1, source_target_pairs={{0,4},{1,5},{2,6},{3,7},{12,8},{13,9},{14,10},{15,11},{16,20},{17,... | collective-permute-start | bytes 3538952 | tf_op jit(solution)/shard_map/ppermute | solution.py:56
  184.9 38.0 %collective-permute-start.27 = (f32[192,384]{1,0:T(8,128)S(1)}, f32[192,384]{1,0:T(8,128)S(1)}, u32[]{:S(2)}, u32[]{:S(2)}) collective-permute-start(f32[192,384]{1,0:T(8,128)S(1)} %constant_dynamic-slice_fusion.33), channel_id=1, source_target_pairs={{0,16},{1,17},{2,18},{3,19},{4,20},{5,21},{6,22},{7,23},{8,24},{9,... | collective-permute-start | bytes 884744 | tf_op jit(solution)/shard_map/ppermute | solution.py:56
  192.4 168.5 %collective-permute-start.82 = (f32[256,1536]{1,0:T(8,128)S(1)}, f32[256,1536]{1,0:T(8,128)S(1)}, u32[]{:S(2)}, u32[]{:S(2)}) collective-permute-start(f32[256,1536]{1,0:T(8,128)S(1)} %slice.248), channel_id=1, source_target_pairs={{0,4},{1,5},{2,6},{3,7},{12,8},{13,9},{14,10},{15,11},{16,20},{17,... | collective-permute-start | bytes 4718600 | tf_op jit(solution)/shard_map/ppermute | solution.py:56
  219.8 119.1 %collective-permute-start.120 = (f32[384,768]{1,0:T(8,128)S(1)}, f32[384,768]{1,0:T(8,128)S(1)}, u32[]{:S(2)}, u32[]{:S(2)}) collective-permute-start(f32[384,768]{1,0:T(8,128)S(1)} %get-tuple-element.56), channel_id=1, source_target_pairs={{0,4},{1,5},{2,6},{3,7},{12,8},{13,9},{14,10},{15,11},{16,20},{17,... | collective-permute-start | bytes 3538952 | tf_op jit(solution)/shard_map/ppermute | solution.py:56
  222.9 60.8 %collective-permute-start.28 = (f32[192,384]{1,0:T(8,128)S(1)}, f32[192,384]{1,0:T(8,128)S(1)}, u32[]{:S(2)}, u32[]{:S(2)}) collective-permute-start(f32[192,384]{1,0:T(8,128)S(1)} %dynamic-slice_add_fusion.21), channel_id=1, source_target_pairs={{0,4},{1,5},{2,6},{3,7},{12,8},{13,9},{14,10},{15,11},{16,20},{17,... | collective-permute-start | bytes 884744 | tf_op jit(solution)/shard_map/ppermute | solution.py:56
  227.3 63.2 %collective-permute-start.18 = (f32[1,200,256]{2,1,0:T(8,128)S(1)}, f32[1,200,256]{2,1,0:T(8,128)S(1)}, u32[]{:S(2)}, u32[]{:S(2)}) collective-permute-start(f32[1,200,256]{2,1,0:T(8,128)S(1)} %select_add_fusion.5), channel_id=1, source_target_pairs={{0,4},{1,5},{2,6},{3,7},{4,8},{5,9},{6,10},{7,11},{8,12},{9,13},{1... | collective-permute-start | bytes 614408 | tf_op jit(solution)/shard_map/ppermute | solution.py:56
  284.6 62.5 %collective-permute-start.111 = (f32[384,768]{1,0:T(8,128)S(1)}, f32[384,768]{1,0:T(8,128)S(1)}, u32[]{:S(2)}, u32[]{:S(2)}) collective-permute-start(f32[384,768]{1,0:T(8,128)S(1)} %get-tuple-element.57), channel_id=1, source_target_pairs={{0,4},{1,5},{2,6},{3,7},{12,8},{13,9},{14,10},{15,11},{16,20},{17,... | collective-permute-start | bytes 3538952 | tf_op jit(solution)/shard_map/ppermute | solution.py:56
  290.5 43.0 %collective-permute-start.54 = (f32[192,768]{1,0:T(8,128)S(1)}, f32[192,768]{1,0:T(8,128)}, u32[]{:S(2)}, u32[]{:S(2)}) collective-permute-start(f32[192,768]{1,0:T(8,128)S(1)} %constant_dynamic-slice_fusion.25), channel_id=1, source_target_pairs={{4,8},{5,9},{6,10},{7,11},{8,4},{9,5},{10,6},{11,7},{20,24},{21,25... | collective-permute-start | bytes 1769480 | tf_op jit(solution)/shard_map/ppermute | solution.py:56
  338.9 99.9 %collective-permute-start.44 = (f32[768,384]{1,0:T(8,128)S(1)}, f32[768,384]{1,0:T(8,128)S(1)}, u32[]{:S(2)}, u32[]{:S(2)}) collective-permute-start(f32[768,384]{1,0:T(8,128)S(1)} %fusion.210), channel_id=1, source_target_pairs={{0,4},{1,5},{2,6},{3,7},{12,8},{13,9},{14,10},{15,11},{16,20},{17,... | collective-permute-start | bytes 3538952 | tf_op jit(solution)/shard_map/ppermute | solution.py:56
  381.3 52.8 %collective-permute-start.58 = (f32[96,768]{1,0:T(8,128)S(1)}, f32[96,768]{1,0:T(8,128)S(1)}, u32[]{:S(2)}, u32[]{:S(2)}) collective-permute-start(f32[96,768]{1,0:T(8,128)S(1)} %pad_maximum_fusion.35), channel_id=1, source_target_pairs={{4,20},{5,21},{6,22},{7,23},{8,24},{9,25},{10,26},{11,27},{20,4},{... | collective-permute-start | bytes 884744 | tf_op jit(solution)/shard_map/ppermute | solution.py:56
  382.1 110.2 %collective-permute-start.83 = (f32[128,1536]{1,0:T(8,128)S(1)}, f32[128,1536]{1,0:T(8,128)S(1)}, u32[]{:S(2)}, u32[]{:S(2)}) collective-permute-start(f32[128,1536]{1,0:T(8,128)S(1)} %constant_dynamic-slice_fusion.15), channel_id=1, source_target_pairs={{4,8},{5,9},{6,10},{7,11},{8,4},{9,5},{10,6},{11,7},{20,24},{21,25... | collective-permute-start | bytes 2359304 | tf_op jit(solution)/shard_map/ppermute | solution.py:56
  383.0 129.6 %collective-permute-start.73 = (f32[128,1536]{1,0:T(8,128)S(1)}, f32[128,1536]{1,0:T(8,128)S(1)}, u32[]{:S(2)}, u32[]{:S(2)}) collective-permute-start(f32[128,1536]{1,0:T(8,128)S(1)} %constant_dynamic-slice_fusion.18), channel_id=1, source_target_pairs={{0,16},{1,17},{2,18},{3,19},{4,20},{5,21},{6,22},{7,23},{8,24},{9,... | collective-permute-start | bytes 2359304 | tf_op jit(solution)/shard_map/ppermute | solution.py:56
  393.1 45.1 %collective-permute-start.37 = (f32[192,384]{1,0:T(8,128)S(1)}, f32[192,384]{1,0:T(8,128)S(1)}, u32[]{:S(2)}, u32[]{:S(2)}) collective-permute-start(f32[192,384]{1,0:T(8,128)S(1)} %dynamic-slice_add_fusion.20), channel_id=1, source_target_pairs={{0,4},{1,5},{2,6},{3,7},{12,8},{13,9},{14,10},{15,11},{16,20},{17,... | collective-permute-start | bytes 884744 | tf_op jit(solution)/shard_map/ppermute | solution.py:56
  438.2 75.8 %collective-permute-start.64 = (f32[128,1536]{1,0:T(8,128)S(1)}, f32[128,1536]{1,0:T(8,128)S(1)}, u32[]{:S(2)}, u32[]{:S(2)}) collective-permute-start(f32[128,1536]{1,0:T(8,128)S(1)} %constant_dynamic-slice_fusion.21), channel_id=1, source_target_pairs={{0,2},{1,3},{2,0},{3,1},{4,6},{5,7},{6,4},{7,5},{8,10},{9,11},{10,... | collective-permute-start | bytes 2359304 | tf_op jit(solution)/shard_map/ppermute | solution.py:56
  453.4 150.4 %collective-permute-start.34 = (f32[768,384]{1,0:T(8,128)S(1)}, f32[768,384]{1,0:T(8,128)S(1)}, u32[]{:S(2)}, u32[]{:S(2)}) collective-permute-start(f32[768,384]{1,0:T(8,128)S(1)} %pad_maximum_fusion.7), channel_id=1, source_target_pairs={{0,1},{1,0},{2,3},{3,2},{4,5},{5,4},{6,7},{7,6},{8,9},{9,8},{10,11... | collective-permute-start | bytes 3538952 | tf_op jit(solution)/shard_map/ppermute | solution.py:56
  456.4 51.3 %collective-permute-start.95 = (f32[96,768]{1,0:T(8,128)S(1)}, f32[96,768]{1,0:T(8,128)S(1)}, u32[]{:S(2)}, u32[]{:S(2)}) collective-permute-start(f32[96,768]{1,0:T(8,128)S(1)} %dynamic-slice_add_fusion.17), channel_id=1, source_target_pairs={{0,4},{1,5},{2,6},{3,7},{12,8},{13,9},{14,10},{15,11},{16,20},{17,... | collective-permute-start | bytes 884744 | tf_op jit(solution)/shard_map/ppermute | solution.py:56
  525.6 132.3 %collective-permute-start.60 = (f32[384,768]{1,0:T(8,128)S(1)}, f32[384,768]{1,0:T(8,128)S(1)}, u32[]{:S(2)}, u32[]{:S(2)}) collective-permute-start(f32[384,768]{1,0:T(8,128)S(1)} %pad_maximum_fusion.10), channel_id=1, source_target_pairs={{4,0},{5,1},{6,2},{7,3},{8,12},{9,13},{10,14},{11,15},{20,16},{21,... | collective-permute-start | bytes 3538952 | tf_op jit(solution)/shard_map/ppermute | solution.py:56
  531.6 59.4 %collective-permute-start.98 = (f32[96,768]{1,0:T(8,128)S(1)}, f32[96,768]{1,0:T(8,128)S(1)}, u32[]{:S(2)}, u32[]{:S(2)}) collective-permute-start(f32[96,768]{1,0:T(8,128)S(1)} %pad_maximum_fusion.36), channel_id=1, source_target_pairs={{4,0},{5,1},{6,2},{7,3},{8,12},{9,13},{10,14},{11,15},{20,16},{21,... | collective-permute-start | bytes 884744 | tf_op jit(solution)/shard_map/ppermute | solution.py:56
  533.8 60.3 %collective-permute-start.107 = (f32[96,768]{1,0:T(8,128)S(1)}, f32[96,768]{1,0:T(8,128)S(1)}, u32[]{:S(2)}, u32[]{:S(2)}) collective-permute-start(f32[96,768]{1,0:T(8,128)S(1)} %pad_maximum_fusion.37), channel_id=1, source_target_pairs={{4,0},{5,1},{6,2},{7,3},{8,12},{9,13},{10,14},{11,15},{20,16},{21,... | collective-permute-start | bytes 884744 | tf_op jit(solution)/shard_map/ppermute | solution.py:56
  535.2 113.1 %collective-permute-start.117 = (f32[192,768]{1,0:T(8,128)S(1)}, f32[192,768]{1,0:T(8,128)S(1)}, u32[]{:S(2)}, u32[]{:S(2)}) collective-permute-start(f32[192,768]{1,0:T(8,128)S(1)} %pad_maximum_fusion.25), channel_id=1, source_target_pairs={{4,8},{5,9},{6,10},{7,11},{8,4},{9,5},{10,6},{11,7},{20,24},{21,25... | collective-permute-start | bytes 1769480 | tf_op jit(solution)/shard_map/ppermute | solution.py:56
  591.0 58.1 %collective-permute-start.126 = (f32[192,768]{1,0:T(8,128)S(1)}, f32[192,768]{1,0:T(8,128)S(1)}, u32[]{:S(2)}, u32[]{:S(2)}) collective-permute-start(f32[192,768]{1,0:T(8,128)S(1)} %pad_maximum_fusion.26), channel_id=1, source_target_pairs={{4,8},{5,9},{6,10},{7,11},{8,4},{9,5},{10,6},{11,7},{20,24},{21,25... | collective-permute-start | bytes 1769480 | tf_op jit(solution)/shard_map/ppermute | solution.py:56
  655.0 107.5 %collective-permute-start.118 = (f32[384,768]{1,0:T(8,128)S(1)}, f32[384,768]{1,0:T(8,128)S(1)}, u32[]{:S(2)}, u32[]{:S(2)}) collective-permute-start(f32[384,768]{1,0:T(8,128)S(1)} %pad_maximum_fusion.13), channel_id=1, source_target_pairs={{4,0},{5,1},{6,2},{7,3},{8,12},{9,13},{10,14},{11,15},{20,16},{21,... | collective-permute-start | bytes 3538952 | tf_op jit(solution)/shard_map/ppermute | solution.py:56
  656.4 106.9 %collective-permute-start.127 = (f32[384,768]{1,0:T(8,128)S(1)}, f32[384,768]{1,0:T(8,128)S(1)}, u32[]{:S(2)}, u32[]{:S(2)}) collective-permute-start(f32[384,768]{1,0:T(8,128)S(1)} %pad_maximum_fusion.14), channel_id=1, source_target_pairs={{4,0},{5,1},{6,2},{7,3},{8,12},{9,13},{10,14},{11,15},{20,16},{21,... | collective-permute-start | bytes 3538952 | tf_op jit(solution)/shard_map/ppermute | solution.py:56
  657.9 81.8 %collective-permute-start.50 = (f32[384,384]{1,0:T(8,128)S(1)}, f32[384,384]{1,0:T(8,128)S(1)}, u32[]{:S(2)}, u32[]{:S(2)}) collective-permute-start(f32[384,384]{1,0:T(8,128)S(1)} %pad_maximum_fusion.21), channel_id=1, source_target_pairs={{4,8},{5,9},{6,10},{7,11},{8,4},{9,5},{10,6},{11,7},{20,24},{21,25... | collective-permute-start | bytes 1769480 | tf_op jit(solution)/shard_map/ppermute | solution.py:56
  660.8 104.0 %collective-permute-start.43 = (f32[768,384]{1,0:T(8,128)S(1)}, f32[768,384]{1,0:T(8,128)S(1)}, u32[]{:S(2)}, u32[]{:S(2)}) collective-permute-start(f32[768,384]{1,0:T(8,128)S(1)} %pad_maximum_fusion.8), channel_id=1, source_target_pairs={{0,1},{1,0},{2,3},{3,2},{4,5},{5,4},{6,7},{7,6},{8,9},{9,8},{10,11... | collective-permute-start | bytes 3538952 | tf_op jit(solution)/shard_map/ppermute | solution.py:56
  662.9 66.4 %collective-permute-start.78 = (f32[64,1536]{1,0:T(8,128)S(1)}, f32[64,1536]{1,0:T(8,128)S(1)}, u32[]{:S(2)}, u32[]{:S(2)}) collective-permute-start(f32[64,1536]{1,0:T(8,128)S(1)} %pad_maximum_fusion.30), channel_id=1, source_target_pairs={{4,0},{5,1},{6,2},{7,3},{8,12},{9,13},{10,14},{11,15},{20,16},{21,... | collective-permute-start | bytes 1179656 | tf_op jit(solution)/shard_map/ppermute | solution.py:56
  763.3 33.7 %collective-permute-start.51 = (f32[768,384]{1,0:T(8,128)S(1)}, f32[768,384]{1,0:T(8,128)S(1)}, u32[]{:S(2)}, u32[]{:S(2)}) collective-permute-start(f32[768,384]{1,0:T(8,128)S(1)} %pad_maximum_fusion.9), channel_id=1, source_target_pairs={{4,0},{5,1},{6,2},{7,3},{8,12},{9,13},{10,14},{11,15},{20,16},{21,... | collective-permute-start | bytes 3538952 | tf_op jit(solution)/shard_map/ppermute | solution.py:56
  764.8 65.3 %collective-permute-start.89 = (f32[256,1536]{1,0:T(8,128)S(1)}, f32[256,1536]{1,0:T(8,128)S(1)}, u32[]{:S(2)}, u32[]{:S(2)}) collective-permute-start(f32[256,1536]{1,0:T(8,128)S(1)} %pad_maximum_fusion.6), channel_id=1, source_target_pairs={{4,0},{5,1},{6,2},{7,3},{8,12},{9,13},{10,14},{11,15},{20,16},{21,... | collective-permute-start | bytes 4718600 | tf_op jit(solution)/shard_map/ppermute | solution.py:56
  790.8 41.4 %collective-permute-start.81 = (f32[256,1536]{1,0:T(8,128)S(1)}, f32[256,1536]{1,0:T(8,128)S(1)}, u32[]{:S(2)}, u32[]{:S(2)}) collective-permute-start(f32[256,1536]{1,0:T(8,128)S(1)} %pad_maximum_fusion.5), channel_id=1, source_target_pairs={{0,1},{1,0},{2,3},{3,2},{4,5},{5,4},{6,7},{7,6},{8,9},{9,8},{10,11... | collective-permute-start | bytes 4718600 | tf_op jit(solution)/shard_map/ppermute | solution.py:56
  797.0 35.4 %collective-permute-start.72 = (f32[256,1536]{1,0:T(8,128)S(1)}, f32[256,1536]{1,0:T(8,128)S(1)}, u32[]{:S(2)}, u32[]{:S(2)}) collective-permute-start(f32[256,1536]{1,0:T(8,128)S(1)} %pad_maximum_fusion.4), channel_id=1, source_target_pairs={{0,1},{1,0},{2,3},{3,2},{4,5},{5,4},{6,7},{7,6},{8,9},{9,8},{10,11... | collective-permute-start | bytes 4718600 | tf_op jit(solution)/shard_map/ppermute | solution.py:56
  (177 other events, 1513.8 us)
